TPU v7x, 256 devices: a whole 4x4x8 slice. The times are simulated.
256 devices in a mesh: dp: 32 (over y_hi, z, core), tensor: 8 (over x, y_lo).
Axes of the slice: x: 4, y: 4 (y_hi: 2, y_lo: 2; y = y_hi * 2 + y_lo), z: 8, core: 2. Of those that a mesh axis runs over, the one named last changes fastest.
Arguments:
- tokens: bfloat16 [32768, 3072], P(('dp', 'tensor')), may hold values from -40 to 40
- indices: int32 [16384], P(('dp', 'tensor')), may hold values from 0 to 127
- gate_weight: bfloat16 [3072, 8192], P(None, 'tensor'), may hold values from -0.109375 to 0.109375
- up_weight: bfloat16 [3072, 8192], P(None, 'tensor'), may hold values from -0.109375 to 0.109375
Outputs:
- input_factor: float32 [384, 3072], P('dp', 'tensor')
- hidden_factor: float32 [1024, 8192], P('dp', 'tensor')
All inputs are finite; a program needn't handle non-finite values.
Results may differ from a plain program's by a relative error of at most 0.0014.
Values may be sent and summed in bfloat16 or wider, within the bound.
A program may use at most 128 MiB of HBM per device.

v0:
```python
import jax
import jax.numpy as jnp
from jax import lax
from jax.sharding import PartitionSpec as P

IBLK = 384


def local(tokens, indices, gate_weight, up_weight):
    groups = lax.axis_size("tensor")
    replicas = lax.axis_size("dp")
    seq_rows = tokens.shape[0]
    per_device = indices.shape[0]
    shards = lax.all_gather(tokens, "tensor", axis=0, tiled=True)
    all_ids = lax.all_gather(indices, "tensor", axis=0, tiled=True)
    source = jnp.arange(groups * per_device, dtype=jnp.int32) // per_device
    sampled = jnp.take(shards, source * seq_rows + all_ids, axis=0)
    row_total = sampled.shape[0]
    inverse_count = 1.0 / (row_total * replicas)
    model_width = tokens.shape[1]
    blocks_here = model_width // (groups * IBLK)
    first_col = lax.axis_index("tensor") * (blocks_here * IBLK)
    owned_flat = lax.dynamic_slice_in_dim(sampled, first_col, blocks_here * IBLK, 1)
    owned_cols = owned_flat.reshape(row_total, blocks_here, IBLK)
    input_share = IBLK // replicas
    piece_cols = owned_cols
    partial_sum = jnp.einsum(
        "rbi,rbj->ibj", piece_cols, owned_cols, preferred_element_type=jnp.float32
    )
    input_factor = lax.psum_scatter(
        partial_sum.reshape(lax.axis_size("dp") * input_share, blocks_here * IBLK) * inverse_count,
        "dp",
        scatter_dimension=0,
        tiled=True,
    )
    gate_pre = jnp.dot(sampled, gate_weight, preferred_element_type=jnp.float32)
    up_pre = jnp.dot(sampled, up_weight, preferred_element_type=jnp.float32)
    hidden = (jax.nn.silu(gate_pre) * up_pre).astype(jnp.bfloat16)
    piece_cols = hidden
    partial_sum = lax.dot_general(
        piece_cols, hidden, (((0,), (0,)), ((), ())), preferred_element_type=jnp.float32
    )
    hidden_factor = lax.psum_scatter(
        partial_sum * inverse_count, "dp", scatter_dimension=0, tiled=True
    )
    return (input_factor, hidden_factor)


def solution(mesh):
    in_specs = (
        P(("dp", "tensor"), None),
        P(("dp", "tensor")),
        P(None, "tensor"),
        P(None, "tensor"),
    )
    out_specs = (P("dp", "tensor"), P("dp", "tensor"))
    return jax.shard_map(local, mesh=mesh, in_specs=in_specs, out_specs=out_specs, check_vma=False)
```

profile of v0, /device:TPU:1, one launch (start us, length us, event | category | flops | bytes accessed | tf_op | source)
XLA Modules:
  0.0 549.0 jit_solution(11676869256479154843)
XLA Ops:
  7.2 0.0 all-gather.2.cloned.1.call-start
  7.2 0.7 all-gather.2.cloned.1.call-update
  7.9 0.0 all-reduce.4.cloned.1.call-start
  7.9 1.3 dynamic-slice
  9.9 0.9 dynamic-update-slice
  10.7 9.6 %all-reduce = s32[512]{0:T(512)S(1)} all-reduce(s32[512]{0:T(512)S(1)} %dynamic-update-slice), channel_id=1, replica_groups=mesh['dp'=32,'tensor'=8] {'tensor'}, use_global_device_ids=true, to_apply=%add | all-reduce | flops 512 | bytes 4096
  20.4 124.8 %all-gather.2.cloned.1.call-done = bf16[1024,3072]{1,0:T(8,128)(2,1)} async-done(((bf16[128,3072]{1,0:T(8,128)(2,1)}), bf16[1024,3072]{1,0:T(8,128)(2,1)}) %all-gather.2.cloned.1.call-update) | async-done | bytes 6291472 | tf_op jit(solution)/shard_map/all_gather | solution.py:14
  145.2 9.7 %gather_fusion = bf16[512,3072]{1,0:T(8,128)(2,1)S(1)} fusion(bf16[1024,3072]{1,0:T(8,128)(2,1)} %all-gather.2.cloned.1.call-done, s32[1024]{0:T(1024)S(1)} %pad_clamp_fusion), kind=kCustom, calls=%fused_computation | custom fusion | bytes 6293504 | tf_op jit(solution)/shard_map/jit(_take)/gather | solution.py:17
  154.9 0.4 broadcast_select_fusion
  155.3 0.0 copy-start
  155.3 1.6 copy-done
  156.9 1.2 fusion
  158.1 0.0 all-reduce.4.cloned.1.call-update
  158.2 0.0 copy-start.1
  158.2 0.2 reduce-scatter.3.cloned.1.call-start
  158.4 8.6 %fusion.9 = f32[512,1024]{1,0:T(8,128)} fusion(bf16[512,3072]{1,0:T(8,128)(2,1)} %copy-done, bf16[3072,1024]{1,0:T(8,128)(2,1)} %param.6), kind=kOutput, calls=%fused_computation.22 | convolution fusion | flops 3221225472 | bytes 11534336 | tf_op jit(solution)/shard_map/dot_general | solution.py:36
  167.0 0.0 copy-done.1
  167.0 15.9 %convolution_multiply_fusion = f32[1024,1024]{1,0:T(8,128)} fusion(f32[512,1024]{1,0:T(8,128)} %fusion.9, bf16[512,3072]{1,0:T(8,128)(2,1)S(1)} %copy-done.1, bf16[3072,1024]{1,0:T(8,128)(2,1)} %param.7), kind=kOutput, calls=%fused_computation.2 | convolution fusion | flops 4299161600 | bytes 15728640 | tf_op jit(solution)/shard_map/dot_general | solution.py:40
  183.0 0.0 copy-start.2
  183.0 0.0 reduce-scatter.3.cloned.1.call-update
  183.0 0.6 copy-done.2
  183.6 0.6 dynamic-slice.1
  184.9 230.5 %all-reduce.4.cloned.1.call-done = f32[384,384]{0,1:T(8,128)} async-done(((f32[384,384]{0,1:T(8,128)}), f32[384,384]{0,1:T(8,128)}) %all-reduce.4.cloned.1.call-update) | async-done | bytes 589840
  415.3 1.1 constant_dynamic-slice_fusion
  416.5 0.7 copy.7
  417.2 125.3 %reduce-scatter.3.cloned.1.call-done = f32[32,1024]{1,0:T(8,128)} async-done(((f32[1024,1024]{1,0:T(8,128)}), f32[32,1024]{1,0:T(8,128)}) %reduce-scatter.3.cloned.1.call-update) | async-done | bytes 131088 | tf_op jit(solution)/shard_map/reduce_scatter | solution.py:43
  (3 shorter events, 0.0 us)
Async XLA Ops:
  7.2 138.0 %all-gather.2.cloned.1.call-start = ((), (), s32[]{:S(2)}) async-start(), calls=%async_computation.1 | async-start | bytes 7077888 | tf_op jit(solution)/shard_map/all_gather | solution.py:14
  7.9 407.4 %all-reduce.4.cloned.1.call-start = ((), (), s32[]{:S(2)}) async-start(), calls=%async_computation.3 | async-start | bytes 1179648
  155.3 1.6 copy-start
  158.2 8.9 %copy-start.1 = (bf16[512,3072]{1,0:T(8,128)(2,1)S(1)}, bf16[512,3072]{1,0:T(8,128)(2,1)}, u32[]{:S(2)}) copy-start(bf16[512,3072]{1,0:T(8,128)(2,1)} %copy-done) | copy-start | bytes 9437188
  158.2 384.3 %reduce-scatter.3.cloned.1.call-start = ((), (), s32[]{:S(2)}) async-start(), calls=%async_computation.2 | async-start | bytes 4325376 | tf_op jit(solution)/shard_map/reduce_scatter | solution.py:43
  183.0 0.7 copy-start.2
Sparse Core Ops, SparseCore 0:
  9.8 135.3 all-gather.1
  158.3 257.0 all-reduce.3
  420.7 121.6 reduce-scatter.2
where the time goes:
time: 553 us; the launch traced here: 549 us
  waiting for transfers between devices  481 us (87%)
  matrix products  25.8 us (5%)
  local copies, waits for them, and re-layouts  16.5 us (3%)
  between operations  15.1 us (3%)
  blocking collectives  9.6 us (2%)
    unnamed x4, waiting for transfers between devices  231 us
    reduce_scatter x1, waiting for transfers between devices, local(): lax.psum_scatter(partial_sum * inverse_count, 'dp', scatter_dimension=0,...  125 us
    all_gather x1, waiting for transfers between devices, local(): shards = lax.all_gather(tokens, 'tensor', axis=0, tiled=True)  125 us
    dot_general x1, matrix products, local(): lax.dot_general(piece_cols, hidden, (((0,), (0,)), ((), ())), preferred_e...  15.9 us
  transfers between devices with their start and end apart: 3, of which 3 were waited for; matrix products, arithmetic and copies ran while one was open for 5% of the time, Pallas kernels for 0%

commit v1 on v0

v1 whole, which is shorter than its diff:
```python
import jax
import jax.numpy as jnp
from jax import lax
from jax.experimental import pallas as pl
from jax.experimental.pallas import tpu as pltpu
from jax.sharding import PartitionSpec as P

D = 3072
UNITS = 1024
IBLK = 384
SAMP = 64
SEQ = 128
ROWS = 512
CHUNKS = 4
KC = D // CHUNKS
TILE = 256
NT = UNITS // TILE
OWN_ROWS = 32
IN_ROWS = 12
IN_PAD = 16
DZ = (4, 3, 5, 2, 6, 1, 7, 0)
INV = 1.0 / 16384
MESH = pl.DeviceIdType.MESH
F32 = jnp.float32
BF16 = jnp.bfloat16

S_OWN, S_XM, S_XP, S_X2, S_Y, S_YXM, S_YXP, S_YX2 = (64 * i for i in range(8))
MSGS = (
    (S_OWN, S_XM, 0, 64, "xp"),
    (S_OWN, S_XP, 0, 64, "xm"),
    (S_OWN, S_Y, 0, 64, "y"),
    (S_XM, S_X2, 0, 32, "xp"),
    (S_XP, S_X2, 32, 32, "xm"),
    (S_XM, S_YXM, 0, 64, "y"),
    (S_XP, S_YXP, 0, 64, "y"),
    (S_X2, S_YX2, 0, 32, "y"),
    (S_YXM, S_YX2, 32, 16, "xp"),
    (S_YXP, S_YX2, 48, 16, "xm"),
)
NM = len(MSGS)


def kernel(
    idx_ref, tok_hbm, wg_hbm, wu_hbm, oin_ref, oh_ref,
    tok, wg, wu, x, accg, accu, h, hs, sel, hts, g, insel, gin, gin_s, gin_sib,
    gin_y, inz, inz_r, ys, yr, zs, zr,
    tok_sem, w_sem, ag_s, ag_r, h_s, h_r, y_s, y_r, z_s, z_r, in_s, in_r, inz_s, inz_rs,
):
    dp = lax.axis_index("dp")
    t = lax.axis_index("tensor")
    yhi = dp // 16
    z = (dp // 2) % 8
    core = dp % 2
    xx = t // 2
    ylo = t % 2
    yhi_p = yhi + core * (1 - 2 * yhi)
    sib = (dp + 1 - 2 * core, t)
    ypart = (yhi_p * 16 + z * 2 + core, xx * 2 + 1 - ylo)
    yfar = (dp + 16 - 32 * yhi, t)
    where = {
        "xp": (dp, lax.rem(xx + 1, 4) * 2 + ylo),
        "xm": (dp, lax.rem(xx + 3, 4) * 2 + ylo),
        "y": ypart,
    }
    zpeer = [(yhi * 16 + lax.rem(z + d, 8) * 2 + core, t) for d in DZ[:7]]

    tcopy = pltpu.make_async_copy(tok_hbm, tok, tok_sem)
    tcopy.start()
    wcopies = []
    for c in range(CHUNKS):
        rows = pl.ds(c * KC, KC)
        pair = (
            pltpu.make_async_copy(wg_hbm.at[rows, :], wg.at[rows, :], w_sem.at[c, 0]),
            pltpu.make_async_copy(wu_hbm.at[rows, :], wu.at[rows, :], w_sem.at[c, 1]),
        )
        for cp in pair:
            cp.start()
        wcopies.append(pair)

    barrier = pltpu.get_barrier_semaphore()
    peers = [where["xp"], where["xm"], ypart, sib, yfar] + zpeer
    for peer in peers:
        pl.semaphore_signal(barrier, inc=1, device_id=peer, device_id_type=MESH)

    pick = (lax.broadcasted_iota(jnp.int32, (SEQ, SAMP), 0) == idx_ref[...]).astype(BF16)
    tcopy.wait()
    for c in range(CHUNKS):
        x[c, pl.ds(S_OWN, 64), :] = lax.dot_general(
            pick, tok[:, c * KC:(c + 1) * KC], (((0,), (0,)), ((), ())),
            preferred_element_type=F32,
        ).astype(BF16)

    pl.semaphore_wait(barrier, len(peers))

    def message(c, m):
        src, dst, first, n, way = MSGS[m]
        return pltpu.make_async_remote_copy(
            src_ref=x.at[c, pl.ds(src + first, n), :],
            dst_ref=x.at[c, pl.ds(dst + first, n), :],
            send_sem=ag_s.at[c, m],
            recv_sem=ag_r.at[c, m],
            device_id=where[way],
            device_id_type=MESH,
        )

    msgs = [[message(c, m) for m in range(NM)] for c in range(CHUNKS)]

    def first_sends(c):
        for m in (0, 1, 2):
            msgs[c][m].start()

    def forwards(c):
        msgs[c][0].wait_recv()
        msgs[c][3].start()
        msgs[c][5].start()
        msgs[c][1].wait_recv()
        msgs[c][4].start()
        msgs[c][6].start()

    def last_forwards(c):
        msgs[c][3].wait_recv()
        msgs[c][7].start()
        msgs[c][5].wait_recv()
        msgs[c][8].start()
        msgs[c][6].wait_recv()
        msgs[c][9].start()

    def arrived(c):
        for m in (2, 4, 7, 8, 9):
            msgs[c][m].wait_recv()
        for cp in wcopies[c]:
            cp.wait()

    def multiply(c):
        rows = pl.ds(c * KC, KC)

        @pl.loop(0, NT)
        def _(n):
            cols = pl.ds(pl.multiple_of(n * TILE, TILE), TILE)
            pg = jnp.dot(x[c], wg[rows, cols], preferred_element_type=F32)
            pu = jnp.dot(x[c], wu[rows, cols], preferred_element_type=F32)
            if c == 0:
                accg[n] = pg
                accu[n] = pu
            elif c < CHUNKS - 1:
                accg[n] += pg
                accu[n] += pu
            else:
                gate = accg[n] + pg
                up = accu[n] + pu
                h[n] = (gate / (1.0 + jnp.exp(-gate)) * up).astype(BF16)

    for c in range(CHUNKS):
        first_sends(c)

    col = lax.broadcasted_iota(jnp.int32, (OWN_ROWS, UNITS), 1)
    row = lax.broadcasted_iota(jnp.int32, (OWN_ROWS, UNITS), 0)
    icol = lax.broadcasted_iota(jnp.int32, (IN_PAD, IBLK), 1)
    irow = lax.broadcasted_iota(jnp.int32, (IN_PAD, IBLK), 0)
    for r in range(16):
        to_y = (1 - yhi) if r < 8 else yhi
        owner = to_y * 16 + lax.rem(z + DZ[r % 8], 8) * 2
        mine = owner + core
        other = owner + 1 - core
        sel[pl.ds(r * OWN_ROWS, OWN_ROWS), :] = (col - mine * OWN_ROWS == row).astype(BF16)
        keep = irow < IN_ROWS
        insel[pl.ds(r * IN_PAD, IN_PAD), :] = ((icol - mine * IN_ROWS == irow) & keep).astype(BF16)
        insel[pl.ds(256 + r * IN_PAD, IN_PAD), :] = ((icol - other * IN_ROWS == irow) & keep).astype(BF16)

    for s in range(CHUNKS + 2):
        if s < CHUNKS:
            forwards(s)
        if 1 <= s <= CHUNKS:
            last_forwards(s - 1)
        if s >= 2:
            arrived(s - 2)
            if s - 2 < CHUNKS - 1:
                multiply(s - 2)

    xb = x[t // 2, :, pl.ds(pl.multiple_of((t % 2) * IBLK, IBLK), IBLK)]
    xt = lax.dot_general(insel[...], xb, (((1,), (1,)), ((), ())), preferred_element_type=F32).astype(BF16)
    gi = jnp.dot(xt, xb, preferred_element_type=F32)
    gin[...] = gi[:256]
    gin_s[...] = gi[256:]
    in_sib = pltpu.make_async_remote_copy(
        src_ref=gin_s, dst_ref=gin_sib, send_sem=in_s.at[0], recv_sem=in_r.at[0],
        device_id=sib, device_id_type=MESH,
    )
    in_sib.start()

    multiply(CHUNKS - 1)
    hcopies = []
    for n in range(NT):
        cp = pltpu.make_async_remote_copy(
            src_ref=h.at[n], dst_ref=hs.at[n], send_sem=h_s.at[n], recv_sem=h_r.at[n],
            device_id=sib, device_id_type=MESH,
        )
        cp.start()
        hcopies.append(cp)

    in_sib.wait_recv()
    gin[...] += gin_sib[...]
    in_y = pltpu.make_async_remote_copy(
        src_ref=gin.at[pl.ds(0, 128)], dst_ref=gin_y, send_sem=in_s.at[1], recv_sem=in_r.at[1],
        device_id=yfar, device_id_type=MESH,
    )
    in_y.start()

    def selected(src):
        total = jnp.zeros((512, ROWS), F32)
        for n in range(NT):
            total += lax.dot_general(
                sel[:, n * TILE:(n + 1) * TILE], src[n], (((1,), (1,)), ((), ())),
                preferred_element_type=F32,
            )
        return total.astype(BF16)

    hts[0] = selected(h)
    for cp in hcopies:
        cp.wait_recv()
    hts[1] = selected(hs)

    def gram(rows):
        @pl.loop(0, NT)
        def _(n):
            g[n, rows, :] = jnp.dot(hts[0, rows, :], h[n], preferred_element_type=F32) + jnp.dot(
                hts[1, rows, :], hs[n], preferred_element_type=F32
            )

    gram(pl.ds(0, 256))
    ycopies = []
    for r in range(8):
        for n in range(NT):
            ys[r, :, n * TILE:(n + 1) * TILE] = g[n, r * OWN_ROWS:(r + 1) * OWN_ROWS, :]
        cp = pltpu.make_async_remote_copy(
            src_ref=ys.at[r], dst_ref=yr.at[r], send_sem=y_s.at[r], recv_sem=y_r.at[r],
            device_id=yfar, device_id_type=MESH,
        )
        cp.start()
        ycopies.append(cp)
    gram(pl.ds(256, 256))

    in_y.wait_recv()
    inzcopies = []
    for r in range(8):
        inz[r] = gin[pl.ds(128 + r * IN_PAD, IN_PAD), :] + gin_y[pl.ds(r * IN_PAD, IN_PAD), :]
        if r < 7:
            cp = pltpu.make_async_remote_copy(
                src_ref=inz.at[r], dst_ref=inz_r.at[r], send_sem=inz_s.at[r], recv_sem=inz_rs.at[r],
                device_id=zpeer[r], device_id_type=MESH,
            )
            cp.start()
            inzcopies.append(cp)

    zcopies = []
    for r in range(8):
        ycopies[r].wait_recv()
        for n in range(NT):
            cols = slice(n * TILE, (n + 1) * TILE)
            zs[r, :, cols] = g[n, 256 + r * OWN_ROWS:256 + (r + 1) * OWN_ROWS, :] + yr[r, :, cols]
        if r < 7:
            cp = pltpu.make_async_remote_copy(
                src_ref=zs.at[r], dst_ref=zr.at[r], send_sem=z_s.at[r], recv_sem=z_r.at[r],
                device_id=zpeer[r], device_id_type=MESH,
            )
            cp.start()
            zcopies.append(cp)

    total = inz[7]
    for r in range(7):
        inzcopies[r].wait_recv()
        total += inz_r[r]
    oin_ref[...] = total[:IN_ROWS] * INV

    total = zs[7]
    for r in range(7):
        zcopies[r].wait_recv()
        total += zr[r]
    oh_ref[...] = total * INV

    for c in range(CHUNKS):
        for m in range(NM):
            msgs[c][m].wait_send()
    for cp in hcopies + ycopies + zcopies + inzcopies + [in_sib, in_y]:
        cp.wait_send()


def local(tokens, indices, gate_weight, up_weight):
    vmem = pltpu.VMEM
    dma = pltpu.SemaphoreType.DMA
    return pl.pallas_call(
        kernel,
        out_shape=(
            jax.ShapeDtypeStruct((IN_ROWS, IBLK), F32),
            jax.ShapeDtypeStruct((OWN_ROWS, UNITS), F32),
        ),
        in_specs=[pl.BlockSpec(memory_space=vmem)] + [pl.BlockSpec(memory_space=pl.ANY)] * 3,
        out_specs=[pl.BlockSpec(memory_space=vmem)] * 2,
        scratch_shapes=[
            vmem((SEQ, D), BF16),
            vmem((D, UNITS), BF16),
            vmem((D, UNITS), BF16),
            vmem((CHUNKS, ROWS, KC), BF16),
            vmem((NT, ROWS, TILE), F32),
            vmem((NT, ROWS, TILE), F32),
            vmem((NT, ROWS, TILE), BF16),
            vmem((NT, ROWS, TILE), BF16),
            vmem((512, UNITS), BF16),
            vmem((2, 512, ROWS), BF16),
            vmem((NT, 512, TILE), F32),
            vmem((512, IBLK), BF16),
            vmem((256, IBLK), F32),
            vmem((256, IBLK), F32),
            vmem((256, IBLK), F32),
            vmem((128, IBLK), F32),
            vmem((8, IN_PAD, IBLK), F32),
            vmem((7, IN_PAD, IBLK), F32),
            vmem((8, OWN_ROWS, UNITS), F32),
            vmem((8, OWN_ROWS, UNITS), F32),
            vmem((8, OWN_ROWS, UNITS), F32),
            vmem((7, OWN_ROWS, UNITS), F32),
            dma,
            dma((CHUNKS, 2)),
            dma((CHUNKS, NM)),
            dma((CHUNKS, NM)),
            dma((NT,)),
            dma((NT,)),
            dma((8,)),
            dma((8,)),
            dma((7,)),
            dma((7,)),
            dma((2,)),
            dma((2,)),
            dma((7,)),
            dma((7,)),
        ],
        compiler_params=pltpu.CompilerParams(
            collective_id=0, has_side_effects=True, vmem_limit_bytes=56 * 2**20
        ),
    )(indices.reshape(1, SAMP), tokens, gate_weight, up_weight)


def solution(mesh):
    in_specs = (
        P(("dp", "tensor"), None),
        P(("dp", "tensor")),
        P(None, "tensor"),
        P(None, "tensor"),
    )
    out_specs = (P("dp", "tensor"), P("dp", "tensor"))
    return jax.shard_map(local, mesh=mesh, in_specs=in_specs, out_specs=out_specs, check_vma=False)
```

time: 553 us -> 82.2 us (0.15)
  waiting for transfers between devices: 481 us -> 0 us
  Pallas kernels: 0 us -> 78.5 us
  matrix products: 25.8 us -> 0 us
  between operations: 15.1 us -> 0.64 us
  local copies, waits for them, and re-layouts: 16.5 us -> 2.91 us
  blocking collectives: 9.6 us -> 0 us
    unnamed x4 -> x0, waiting for transfers between devices: 231 us -> none
    reduce_scatter x1 -> x0, waiting for transfers between devices: 125 us -> none  [local(): lax.psum_scatter(partial_sum * inverse_count, 'dp', scatter_dimension=0,...]
    all_gather x1 -> x0, waiting for transfers between devices: 125 us -> none  [local(): shards = lax.all_gather(tokens, 'tensor', axis=0, tiled=True)]
    pallas_call x0 -> x1, Pallas kernels: none -> 78.5 us  [local(): pl.pallas_call(kernel, out_shape=(jax.ShapeDtypeStruct((IN_ROWS, IBLK), F...]
    dot_general x3 -> x0, matrix products: 25.8 us -> none  [the longest x1 15.9 us: local(): lax.dot_general(piece_cols, hidden, (((0,), (0,)), ((), ())), preferred_e...]
    gather x1 -> x0, local copies, waits for them, and re-layouts: 9.7 us -> none  [local(): sampled = jnp.take(shards, source * seq_rows + all_ids, axis=0)]
    unnamed x1 -> x0, blocking collectives: 9.6 us -> none
  transfers between devices with their start and end apart: 3 -> 0, of which waited for: 3 -> 0; matrix products, arithmetic and copies ran while one was open for 5% -> 0% of each run, Pallas kernels for 0% -> 0%
where the time goes in v1:
time: 82.2 us; the launch traced here: 82 us
  Pallas kernels  78.5 us (95%)
  local copies, waits for them, and re-layouts  2.91 us (4%)
    pallas_call x1, Pallas kernels, local(): pl.pallas_call(kernel, out_shape=(jax.ShapeDtypeStruct((IN_ROWS, IBLK), F...  78.5 us
    unnamed x2, local copies, waits for them, and re-layouts  2.91 us

profile of v1, /device:TPU:1, one launch (start us, length us, event | category | flops | bytes accessed | tf_op | source)
XLA Modules:
  0.0 82.0 jit_solution(11190431777871085916)
XLA Ops:
  0.6 78.5 %shard_map.59 = (f32[12,384]{1,0:T(8,128)}, f32[32,1024]{1,0:T(8,128)}) custom-call(s32[1,64]{1,0:T(1,128)} %bitcast.1, bf16[128,3072]{1,0:T(8,128)(2,1)} %tok_hbm.1, bf16[3072,1024]{1,0:T(8,128)(2,1)} %wg_hbm.1, bf16[3072,1024]{1,0:T(8,128)(2,1)} %wu_hbm.1), custom_call_target="tpu_custom_call" | custom-call | tf_op jit(solution)/shard_map/pallas_call | solution.py:291
  79.1 1.3 %copy.8 = f32[12,384]{1,0:T(8,128)} copy(f32[12,384]{1,0:T(8,128)} %get-tuple-element.4) | data formatting | bytes 36864
  80.4 1.6 %copy.9 = f32[32,1024]{1,0:T(8,128)} copy(f32[32,1024]{1,0:T(8,128)} %get-tuple-element.5) | data formatting | bytes 262144

commit v2 on v1

v2 whole, which is shorter than its diff:
```python
import jax
import jax.numpy as jnp
from jax import lax
from jax.experimental import pallas as pl
from jax.experimental.pallas import tpu as pltpu
from jax.sharding import PartitionSpec as P

D = 3072
UNITS = 1024
IBLK = 384
SAMP = 64
SEQ = 128
ROWS = 512
CHUNKS = 4
KC = D // CHUNKS
TILE = 256
NT = UNITS // TILE
OWN_ROWS = 32
IN_ROWS = 12
IN_PAD = 16
DZ = (4, 3, 5, 2, 6, 1, 7, 0)
INV = 1.0 / 16384
STEPS = 32000.0
MESH = pl.DeviceIdType.MESH
F32 = jnp.float32
BF16 = jnp.bfloat16
I16 = jnp.int16
I32 = jnp.int32

S_OWN, S_XM, S_XP, S_X2, S_Y, S_YXM, S_YXP, S_YX2 = (64 * i for i in range(8))
MSGS = (
    (S_OWN, S_XM, 0, 64, "xp"),
    (S_OWN, S_XP, 0, 64, "xm"),
    (S_OWN, S_Y, 0, 64, "y"),
    (S_XM, S_X2, 0, 32, "xp"),
    (S_XP, S_X2, 32, 32, "xm"),
    (S_XM, S_YXM, 0, 64, "y"),
    (S_XP, S_YXP, 0, 64, "y"),
    (S_X2, S_YX2, 0, 32, "y"),
    (S_YXM, S_YX2, 32, 16, "xp"),
    (S_YXP, S_YX2, 48, 16, "xm"),
)
NM = len(MSGS)


def row_code(vals):
    top = jnp.max(jnp.abs(vals), axis=1, keepdims=True)
    code = jnp.ceil(8.0 * jnp.log2(jnp.maximum(top, 1e-30)))
    q = jnp.round(vals * (jnp.exp2(code * -0.125) * STEPS))
    return q.astype(I32).astype(I16), code.astype(I32)


def row_scale(code):
    return jnp.exp2(code.astype(I32).astype(F32) * 0.125) * (1.0 / STEPS)


def kernel(
    idx_hbm, tok_hbm, wg_hbm, wu_hbm, oin_ref, oh_ref,
    idx, tok, wg, wu, x, accg, accu, h, hs, hts, g, gin, gin_s, gin_sib,
    iys, iyr, izs, izr, ys, yr, zs, zr,
    tok_sem, w_sem, ag_s, ag_r, h_s, h_r, y_s, y_r, z_s, z_r, in_s, in_r, iz_s, iz_r, rel,
):
    dp = lax.axis_index("dp")
    t = lax.axis_index("tensor")
    yhi = dp // 16
    z = (dp // 2) % 8
    core = dp % 2
    xx = t // 2
    ylo = t % 2
    yhi_p = yhi + core * (1 - 2 * yhi)
    sib = (dp + 1 - 2 * core, t)
    ypart = (yhi_p * 16 + z * 2 + core, xx * 2 + 1 - ylo)
    yfar = (dp + 16 - 32 * yhi, t)
    where = {
        "xp": (dp, lax.rem(xx + 1, 4) * 2 + ylo),
        "xm": (dp, lax.rem(xx + 3, 4) * 2 + ylo),
        "y": ypart,
    }

    def zpeer(d):
        return (yhi * 16 + lax.rem(z + d, 8) * 2 + core, t)

    icopy = pltpu.make_async_copy(idx_hbm, idx, tok_sem.at[0])
    icopy.start()
    tcopy = pltpu.make_async_copy(tok_hbm, tok, tok_sem.at[1])
    tcopy.start()

    barrier = pltpu.get_barrier_semaphore()
    peers = [where["xp"], where["xm"], ypart, sib, yfar, zpeer(1), zpeer(7)]
    for peer in peers:
        pl.semaphore_signal(barrier, inc=1, device_id=peer, device_id_type=MESH)

    def wcopy(c):
        rows = pl.ds(pl.multiple_of(c * KC, KC), KC)
        return (
            pltpu.make_async_copy(wg_hbm.at[rows, :], wg.at[rows, :], w_sem.at[c, 0]),
            pltpu.make_async_copy(wu_hbm.at[rows, :], wu.at[rows, :], w_sem.at[c, 1]),
        )

    icopy.wait()
    pick = (lax.broadcasted_iota(I32, (SEQ, SAMP), 0) == idx[...]).astype(BF16)
    tcopy.wait()
    for c in range(CHUNKS):
        x[c, pl.ds(S_OWN, 64), :] = lax.dot_general(
            pick, tok[:, c * KC:(c + 1) * KC], (((0,), (0,)), ((), ())),
            preferred_element_type=F32,
        ).astype(BF16)
    for c in range(CHUNKS):
        for cp in wcopy(c):
            cp.start()

    pl.semaphore_wait(barrier, len(peers))

    def message(c, m):
        src, dst, first, n, way = MSGS[m]
        return pltpu.make_async_remote_copy(
            src_ref=x.at[c, pl.ds(src + first, n), :],
            dst_ref=x.at[c, pl.ds(dst + first, n), :],
            send_sem=ag_s.at[c, m],
            recv_sem=ag_r.at[c, m],
            device_id=where[way],
            device_id_type=MESH,
        )

    def tell(k):
        pl.semaphore_signal(rel.at[k, 0], inc=1, device_id=zpeer(1), device_id_type=MESH)
        pl.semaphore_signal(rel.at[k, 1], inc=1, device_id=zpeer(7), device_id_type=MESH)

    def told(k):
        pl.semaphore_wait(rel.at[k, 0], 1)
        pl.semaphore_wait(rel.at[k, 1], 1)

    def forwards(c):
        message(c, 0).wait_recv()
        message(c, 3).start()
        message(c, 5).start()
        message(c, 1).wait_recv()
        message(c, 4).start()
        message(c, 6).start()

    def last_forwards(c):
        message(c, 3).wait_recv()
        message(c, 7).start()
        message(c, 5).wait_recv()
        message(c, 8).start()
        message(c, 6).wait_recv()
        message(c, 9).start()

    def arrived(c):
        for m in (2, 4, 7, 8, 9):
            message(c, m).wait_recv()
        for cp in wcopy(c):
            cp.wait()

    def products(c, n):
        rows = pl.ds(pl.multiple_of(c * KC, KC), KC)
        cols = pl.ds(pl.multiple_of(n * TILE, TILE), TILE)
        pg = jnp.dot(x[c], wg[rows, cols], preferred_element_type=F32)
        pu = jnp.dot(x[c], wu[rows, cols], preferred_element_type=F32)
        return pg, pu

    for c in range(CHUNKS):
        for m in (0, 1, 2):
            message(c, m).start()
    tell(0)

    accg[...] = jnp.zeros_like(accg)
    accu[...] = jnp.zeros_like(accu)

    forwards(0)
    told(0)
    tell(1)
    forwards(1)
    last_forwards(0)
    told(1)
    tell(2)

    @pl.loop(0, CHUNKS - 1)
    def _(c):
        @pl.when(c < CHUNKS - 2)
        def _():
            forwards(c + 2)

        last_forwards(c + 1)
        arrived(c)

        @pl.loop(0, NT)
        def _(n):
            pg, pu = products(c, n)
            accg[n] += pg
            accu[n] += pu

    told(2)
    arrived(CHUNKS - 1)

    icol = lax.broadcasted_iota(I32, (IN_PAD, IBLK), 1)
    irow = lax.broadcasted_iota(I32, (IN_PAD, IBLK), 0)

    def in_rows(which):
        parts = []
        for r in range(16):
            to_y = (1 - yhi) if r < 8 else yhi
            owner = to_y * 16 + lax.rem(z + DZ[r % 8], 8) * 2 + which
            parts.append(((icol - owner * IN_ROWS == irow) & (irow < IN_ROWS)).astype(BF16))
        return jnp.concatenate(parts, axis=0)

    xb = x[t // 2, :, pl.ds(pl.multiple_of((t % 2) * IBLK, IBLK), IBLK)]
    for which, dst in ((1 - core, gin_s), (core, gin)):
        xt = lax.dot_general(
            in_rows(which), xb, (((1,), (1,)), ((), ())), preferred_element_type=F32
        ).astype(BF16)
        dst[...] = jnp.dot(xt, xb, preferred_element_type=F32)
    in_sib = pltpu.make_async_remote_copy(
        src_ref=gin_s, dst_ref=gin_sib, send_sem=in_s.at[0], recv_sem=in_r.at[0],
        device_id=sib, device_id_type=MESH,
    )
    in_sib.start()

    def hcopy(n):
        return pltpu.make_async_remote_copy(
            src_ref=h.at[n], dst_ref=hs.at[n], send_sem=h_s.at[n], recv_sem=h_r.at[n],
            device_id=sib, device_id_type=MESH,
        )

    @pl.loop(0, NT)
    def _(n):
        pg, pu = products(CHUNKS - 1, n)
        gate = accg[n] + pg
        up = accu[n] + pu
        h[n] = (gate / (1.0 + jnp.exp(-gate)) * up).astype(BF16)
        hcopy(n).start()

    scol = lax.broadcasted_iota(I32, (128, TILE), 1)
    srow = lax.broadcasted_iota(I32, (128, TILE), 0)
    pick_rows = (scol == (srow // 32) * 64 + core * 32 + srow % 32).astype(BF16)

    def take_rows(src, n, k):
        rows = lax.dot_general(
            pick_rows, src[n], (((1,), (1,)), ((), ())), preferred_element_type=F32
        ).astype(BF16)
        for q in range(4):
            dz = lax.rem((n % 2) * 4 + q + 8 - z, 8)
            place = jnp.where(dz >= 4, 2 * (dz - 4), 7 - 2 * dz)
            place = place + jnp.where(n // 2 == yhi, 8, 0)
            hts[k, pl.ds(pl.multiple_of(place * 32, 32), 32), :] = rows[q * 32:(q + 1) * 32]

    @pl.loop(0, NT)
    def _(n):
        take_rows(h, n, 0)

    @pl.loop(0, NT)
    def _(n):
        g[n] = jnp.dot(hts[0], h[n], preferred_element_type=F32)

    in_sib.wait_recv()
    q, code = row_code(gin[0:128, :] + gin_sib[0:128, :])
    lane = lax.broadcasted_iota(I32, (16, 128), 1)
    packed = jnp.zeros((16, 128), I32)
    for r in range(8):
        for b in range(3):
            iys[3 * r + b] = q[16 * r:16 * r + 16, 128 * b:128 * b + 128]
        packed = jnp.where(lane // 16 == r, code[16 * r:16 * r + 16], packed)
    iys[24] = packed.astype(I16)
    in_y = pltpu.make_async_remote_copy(
        src_ref=iys, dst_ref=iyr, send_sem=in_s.at[1], recv_sem=in_r.at[1],
        device_id=yfar, device_id_type=MESH,
    )
    in_y.start()

    @pl.loop(0, NT)
    def _(n):
        hcopy(n).wait_recv()
        take_rows(hs, n, 1)

    def add_gram(first):
        @pl.loop(0, NT)
        def _(n):
            rows = pl.ds(first, 256)
            g[n, rows, :] += jnp.dot(hts[1, rows, :], hs[n], preferred_element_type=F32)

    def encode(halves, buf):
        codes = []
        for a, vals in enumerate(halves):
            q, code = row_code(vals)
            for b in range(8):
                buf[8 * a + b] = q[:, 128 * b:128 * b + 128]
            codes.append(code)
        buf[16] = jnp.where(lane < 64, codes[0], codes[1]).astype(I16)

    def decode(buf):
        codes = buf[16]
        out = []
        for a in range(2):
            s = row_scale(codes[:, 64 * a:64 * a + 1])
            cat = jnp.concatenate([buf[8 * a + b] for b in range(8)], axis=1)
            out.append(cat.astype(I32).astype(F32) * s)
        return out

    def g_halves(first):
        out = []
        for a in range(2):
            rows = pl.ds(pl.multiple_of(first + 16 * a, 16), 16)
            out.append(jnp.concatenate([g[n, rows, :] for n in range(NT)], axis=1))
        return out

    def ycopy(r):
        return pltpu.make_async_remote_copy(
            src_ref=ys.at[r], dst_ref=yr.at[r], send_sem=y_s.at[r], recv_sem=y_r.at[r],
            device_id=yfar, device_id_type=MESH,
        )

    def far(r):
        k = (r + 1) // 2
        return zpeer(jnp.where(r % 2 == 0, 4 + k, 4 - k))

    def zcopy(r):
        return pltpu.make_async_remote_copy(
            src_ref=zs.at[r], dst_ref=zr.at[r], send_sem=z_s.at[r], recv_sem=z_r.at[r],
            device_id=far(r), device_id_type=MESH,
        )

    def izcopy(r):
        return pltpu.make_async_remote_copy(
            src_ref=izs.at[r], dst_ref=izr.at[r], send_sem=iz_s.at[r], recv_sem=iz_r.at[r],
            device_id=far(r), device_id_type=MESH,
        )

    add_gram(0)

    @pl.loop(0, 8)
    def _(r):
        encode(g_halves(r * 32), ys.at[r])
        ycopy(r).start()

    add_gram(256)

    in_y.wait_recv()
    codes = iyr[24]
    own_in = None
    for r in range(8):
        s = row_scale(codes[:, 16 * r:16 * r + 1])
        rows = pl.ds(128 + 16 * r, 16)
        cat = jnp.concatenate([iyr[3 * r + b] for b in range(3)], axis=1)
        total = gin[rows, :] + gin_sib[rows, :] + cat.astype(I32).astype(F32) * s
        if r < 7:
            q, code = row_code(total)
            for b in range(3):
                izs[r, b] = q[:, 128 * b:128 * b + 128]
            izs[r, 3] = jnp.broadcast_to(code, (16, 128)).astype(I16)
            izcopy(r).start()
        else:
            gin[pl.ds(0, 16), :] = total

    @pl.loop(0, 7)
    def _(r):
        ycopy(r).wait_recv()
        own = g_halves(256 + r * 32)
        got = decode(yr.at[r])
        encode([a + b for a, b in zip(own, got)], zs.at[r])
        zcopy(r).start()

    ycopy(7).wait_recv()
    own = g_halves(256 + 7 * 32)
    got = decode(yr.at[7])
    for a in range(2):
        oh_ref[pl.ds(16 * a, 16), :] = own[a] + got[a]

    total = gin[pl.ds(0, 16), :]
    for r in range(7):
        izcopy(r).wait_recv()
        s = row_scale(izr[r, 3][:, 0:1])
        cat = jnp.concatenate([izr[r, b] for b in range(3)], axis=1)
        total += cat.astype(I32).astype(F32) * s
    oin_ref[...] = total[:IN_ROWS] * INV

    @pl.loop(0, 7)
    def _(r):
        zcopy(r).wait_recv()
        got = decode(zr.at[r])
        last = jnp.where(r == 6, INV, 1.0)
        for a in range(2):
            rows = pl.ds(16 * a, 16)
            oh_ref[rows, :] = (oh_ref[rows, :] + got[a]) * last

    @pl.loop(0, CHUNKS)
    def _(c):
        for m in range(NM):
            message(c, m).wait_send()

    @pl.loop(0, NT)
    def _(n):
        hcopy(n).wait_send()

    @pl.loop(0, 7)
    def _(r):
        ycopy(r).wait_send()
        zcopy(r).wait_send()
        izcopy(r).wait_send()

    ycopy(7).wait_send()
    in_sib.wait_send()
    in_y.wait_send()


def pass_on(a_ref, b_ref, c_ref, d_ref, sem):
    copies = [
        pltpu.make_async_copy(a_ref, c_ref, sem.at[0]),
        pltpu.make_async_copy(b_ref, d_ref, sem.at[1]),
    ]
    for cp in copies:
        cp.start()
    for cp in copies:
        cp.wait()


def local(tokens, indices, gate_weight, up_weight):
    vmem = pltpu.VMEM
    dma = pltpu.SemaphoreType.DMA
    whole = pl.BlockSpec(memory_space=pl.ANY)
    out_shape = (
        jax.ShapeDtypeStruct((IN_ROWS, IBLK), F32),
        jax.ShapeDtypeStruct((OWN_ROWS, UNITS), F32),
    )
    factors = pl.pallas_call(
        kernel,
        out_shape=out_shape,
        in_specs=[whole] * 4,
        out_specs=[pl.BlockSpec(memory_space=vmem)] * 2,
        scratch_shapes=[
            vmem((1, SAMP), I32),
            vmem((SEQ, D), BF16),
            vmem((D, UNITS), BF16),
            vmem((D, UNITS), BF16),
            vmem((CHUNKS, ROWS, KC), BF16),
            vmem((NT, ROWS, TILE), F32),
            vmem((NT, ROWS, TILE), F32),
            vmem((NT, ROWS, TILE), BF16),
            vmem((NT, ROWS, TILE), BF16),
            vmem((2, 512, ROWS), BF16),
            vmem((NT, 512, TILE), F32),
            vmem((256, IBLK), F32),
            vmem((256, IBLK), F32),
            vmem((256, IBLK), F32),
            vmem((25, 16, 128), I16),
            vmem((25, 16, 128), I16),
            vmem((7, 4, 16, 128), I16),
            vmem((7, 4, 16, 128), I16),
            vmem((8, 17, 16, 128), I16),
            vmem((8, 17, 16, 128), I16),
            vmem((7, 17, 16, 128), I16),
            vmem((7, 17, 16, 128), I16),
            dma((2,)),
            dma((CHUNKS, 2)),
            dma((CHUNKS, NM)),
            dma((CHUNKS, NM)),
            dma((NT,)),
            dma((NT,)),
            dma((8,)),
            dma((8,)),
            dma((7,)),
            dma((7,)),
            dma((2,)),
            dma((2,)),
            dma((7,)),
            dma((7,)),
            pltpu.SemaphoreType.REGULAR((3, 2)),
        ],
        compiler_params=pltpu.CompilerParams(
            collective_id=0, has_side_effects=True, vmem_limit_bytes=56 * 2**20
        ),
    )(indices.reshape(1, SAMP), tokens, gate_weight, up_weight)
    return pl.pallas_call(
        pass_on,
        out_shape=out_shape,
        in_specs=[whole] * 2,
        out_specs=[whole] * 2,
        scratch_shapes=[dma((2,))],
    )(*factors)


def solution(mesh):
    in_specs = (
        P(("dp", "tensor"), None),
        P(("dp", "tensor")),
        P(None, "tensor"),
        P(None, "tensor"),
    )
    out_specs = (P("dp", "tensor"), P("dp", "tensor"))
    return jax.shard_map(local, mesh=mesh, in_specs=in_specs, out_specs=out_specs, check_vma=False)
```

time: 82.2 us -> 69.8 us (0.85)
  Pallas kernels: 78.5 us -> 69.1 us
  local copies, waits for them, and re-layouts: 2.91 us -> 0 us
    pallas_call x1 -> x2, Pallas kernels: 78.5 us -> 69.1 us  [the longest x1 63.2 us: local(): pl.pallas_call(kernel, out_shape=out_shape, in_specs=[whole] * 4, out_spe...]
    unnamed x2 -> x0, local copies, waits for them, and re-layouts: 2.91 us -> none
where the time goes in v2:
time: 69.8 us; the launch traced here: 69.7 us
  Pallas kernels  69.1 us (99%)
    pallas_call x1, Pallas kernels, local(): pl.pallas_call(kernel, out_shape=out_shape, in_specs=[whole] * 4, out_spe...  63.2 us
    pallas_call x1, Pallas kernels, local(): pl.pallas_call(pass_on, out_shape=out_shape, in_specs=[whole] * 2, out_sp...  5.84 us

profile of v2, /device:TPU:1, one launch (start us, length us, event | category | flops | bytes accessed | tf_op | source)
XLA Modules:
  0.0 69.7 jit_solution(13114662937453481129)
XLA Ops:
  0.6 63.2 %shard_map.59 = (f32[12,384]{1,0:T(8,128)}, f32[32,1024]{1,0:T(8,128)}) custom-call(s32[1,64]{1,0:T(1,128)} %bitcast.1, bf16[128,3072]{1,0:T(8,128)(2,1)} %tok_hbm.1, bf16[3072,1024]{1,0:T(8,128)(2,1)} %wg_hbm.1, bf16[3072,1024]{1,0:T(8,128)(2,1)} %wu_hbm.1), custom_call_target="tpu_custom_call" | custom-call | tf_op jit(solution)/shard_map/pallas_call | solution.py:424
  63.9 5.8 %shard_map.60 = (f32[12,384]{1,0:T(8,128)}, f32[32,1024]{1,0:T(8,128)}) custom-call(f32[12,384]{1,0:T(8,128)} %get-tuple-element.4.a_ref, f32[32,1024]{1,0:T(8,128)} %get-tuple-element.5.b_ref), custom_call_target="tpu_custom_call" | custom-call | tf_op jit(solution)/shard_map/pallas_call | solution.py:472

commit v3 on v2

v3 whole, which is shorter than its diff:
```python
import jax
import jax.numpy as jnp
from jax import lax
from jax.experimental import pallas as pl
from jax.experimental.pallas import tpu as pltpu
from jax.sharding import PartitionSpec as P

D = 3072
UNITS = 1024
IBLK = 384
SAMP = 64
SEQ = 128
ROWS = 512
CHUNKS = 4
KC = D // CHUNKS
TILE = 512
NT = UNITS // TILE
TURN = 256
OWN_ROWS = 32
IN_ROWS = 12
IN_PAD = 16
DZ = (4, 3, 5, 2, 6, 1, 7, 0)
STEP = (1, 3, 7, 2, 6, 1, 7)
INV = 1.0 / 16384
STEPS = 32000.0
MESH = pl.DeviceIdType.MESH
F32 = jnp.float32
BF16 = jnp.bfloat16
I16 = jnp.int16
I32 = jnp.int32

S_OWN, S_XM, S_XP, S_Y, S_YXM, S_YXP, S_X2, S_YX2 = (64 * i for i in range(8))
HALF = 256
MSGS = (
    (S_OWN, S_XM, 0, 64, "xp"),
    (S_OWN, S_XP, 0, 64, "xm"),
    (S_OWN, S_Y, 0, 64, "y"),
    (S_XM, S_X2, 0, 32, "xp"),
    (S_XP, S_X2, 32, 32, "xm"),
    (S_XM, S_YXM, 0, 64, "y"),
    (S_XP, S_YXP, 0, 64, "y"),
    (S_X2, S_YX2, 0, 32, "y"),
    (S_YXM, S_YX2, 32, 16, "xp"),
    (S_YXP, S_YX2, 48, 16, "xm"),
)
NM = len(MSGS)


def row_code(vals):
    top = jnp.max(jnp.abs(vals), axis=1, keepdims=True)
    code = jnp.ceil(8.0 * jnp.log2(jnp.maximum(top, 1e-30)))
    q = jnp.round(vals * (jnp.exp2(code * -0.125) * STEPS))
    return q.astype(I32).astype(I16), code.astype(I32)


def row_scale(code):
    return jnp.exp2(code.astype(I32).astype(F32) * 0.125) * (1.0 / STEPS)


def kernel(
    idx_hbm, tok_hbm, wg_hbm, wu_hbm, oin_ref, oh_ref,
    idx, tok, wg, wu, x, accg, accu, h1, h2, ht1, ht2, g, insel, gin, gin_sib,
    iys, iyr, izs, izr, ys, yr, fs, fr, zs, zr,
    tok_sem, w_sem, ag_s, ag_r, h_s, h_r, y_s, y_r, f_s, f_r, z_s, z_r, in_s, in_r, iz_s, iz_r, rel,
):
    dp = lax.axis_index("dp")
    t = lax.axis_index("tensor")
    yhi = dp // 16
    z = (dp // 2) % 8
    core = dp % 2
    xx = t // 2
    ylo = t % 2
    yhi_p = yhi + core * (1 - 2 * yhi)
    sib = (dp + 1 - 2 * core, t)
    ypart = (yhi_p * 16 + z * 2 + core, xx * 2 + 1 - ylo)
    yfar = (dp + 16 - 32 * yhi, t)
    where = {
        "xp": (dp, lax.rem(xx + 1, 4) * 2 + ylo),
        "xm": (dp, lax.rem(xx + 3, 4) * 2 + ylo),
        "y": ypart,
    }

    def zpeer(d):
        return (yhi * 16 + lax.rem(z + d, 8) * 2 + core, t)

    icopy = pltpu.make_async_copy(idx_hbm, idx, tok_sem.at[0])
    icopy.start()
    tcopy = pltpu.make_async_copy(tok_hbm, tok, tok_sem.at[1])
    tcopy.start()

    barrier = pltpu.get_barrier_semaphore()
    peers = [where["xp"], where["xm"], ypart, sib, yfar, zpeer(1), zpeer(7)]
    for peer in peers:
        pl.semaphore_signal(barrier, inc=1, device_id=peer, device_id_type=MESH)

    def wcopy(c):
        rows = pl.ds(pl.multiple_of(c * KC, KC), KC)
        return (
            pltpu.make_async_copy(wg_hbm.at[rows, :], wg.at[rows, :], w_sem.at[c, 0]),
            pltpu.make_async_copy(wu_hbm.at[rows, :], wu.at[rows, :], w_sem.at[c, 1]),
        )

    icopy.wait()
    pick = (lax.broadcasted_iota(I32, (SEQ, SAMP), 0) == idx[...]).astype(BF16)
    tcopy.wait()
    for c in range(CHUNKS):
        x[c, pl.ds(S_OWN, 64), :] = lax.dot_general(
            pick, tok[:, c * KC:(c + 1) * KC], (((0,), (0,)), ((), ())),
            preferred_element_type=F32,
        ).astype(BF16)
    for c in range(CHUNKS):
        for cp in wcopy(c):
            cp.start()

    pl.semaphore_wait(barrier, len(peers))

    def message(c, m):
        src, dst, first, n, way = MSGS[m]
        return pltpu.make_async_remote_copy(
            src_ref=x.at[c, pl.ds(src + first, n), :],
            dst_ref=x.at[c, pl.ds(dst + first, n), :],
            send_sem=ag_s.at[c, m],
            recv_sem=ag_r.at[c, m],
            device_id=where[way],
            device_id_type=MESH,
        )

    def tell(k):
        pl.semaphore_signal(rel.at[k, 0], inc=1, device_id=zpeer(1), device_id_type=MESH)
        pl.semaphore_signal(rel.at[k, 1], inc=1, device_id=zpeer(7), device_id_type=MESH)

    def told(k):
        pl.semaphore_wait(rel.at[k, 0], 1)
        pl.semaphore_wait(rel.at[k, 1], 1)

    def forwards(c):
        message(c, 0).wait_recv()
        message(c, 3).start()
        message(c, 5).start()
        message(c, 1).wait_recv()
        message(c, 4).start()
        message(c, 6).start()

    def last_forwards(c):
        message(c, 3).wait_recv()
        message(c, 7).start()
        message(c, 5).wait_recv()
        message(c, 8).start()
        message(c, 6).wait_recv()
        message(c, 9).start()

    def products(c, group):
        mine = pl.ds(group * HALF, HALF)
        rows = pl.ds(pl.multiple_of(c * KC, KC), KC)

        @pl.loop(0, NT)
        def _(n):
            cols = pl.ds(pl.multiple_of(n * TILE, TILE), TILE)
            accg[n, mine, :] += jnp.dot(x[c, mine, :], wg[rows, cols], preferred_element_type=F32)
            accu[n, mine, :] += jnp.dot(x[c, mine, :], wu[rows, cols], preferred_element_type=F32)

    hidden = (h1, h2)
    turned = (ht1, ht2)

    def hcopy(group, n):
        ref = hidden[group]
        cols = pl.ds(pl.multiple_of(n * TILE, TILE), TILE)
        return pltpu.make_async_remote_copy(
            src_ref=ref.at[pl.ds(0, HALF), cols], dst_ref=ref.at[pl.ds(HALF, HALF), cols],
            send_sem=h_s.at[group, n], recv_sem=h_r.at[group, n],
            device_id=sib, device_id_type=MESH,
        )

    def finish(group):
        mine = pl.ds(group * HALF, HALF)
        rows = pl.ds((CHUNKS - 1) * KC, KC)

        @pl.loop(0, NT)
        def _(n):
            cols = pl.ds(pl.multiple_of(n * TILE, TILE), TILE)
            last = x[CHUNKS - 1, mine, :]
            gate = accg[n, mine, :] + jnp.dot(last, wg[rows, cols], preferred_element_type=F32)
            up = accu[n, mine, :] + jnp.dot(last, wu[rows, cols], preferred_element_type=F32)
            hidden[group][pl.ds(0, HALF), cols] = (gate / (1.0 + jnp.exp(-gate)) * up).astype(BF16)
            hcopy(group, n).start()

    scol = lax.broadcasted_iota(I32, (128, TURN), 1)
    srow = lax.broadcasted_iota(I32, (128, TURN), 0)
    pick_rows = (scol == (srow // 32) * 64 + core * 32 + srow % 32).astype(BF16)

    def take_rows(group, first, count):
        src = pl.ds(first, count)

        for n in range(UNITS // TURN):
            rows = lax.dot_general(
                pick_rows, hidden[group][src, n * TURN:(n + 1) * TURN], (((1,), (1,)), ((), ())),
                preferred_element_type=F32,
            ).astype(BF16)
            for q in range(4):
                dz = lax.rem((n % 2) * 4 + q + 8 - z, 8)
                place = jnp.where(dz >= 4, 2 * (dz - 4), 7 - 2 * dz)
                place = place + jnp.where(n // 2 == yhi, 8, 0)
                to = pl.ds(pl.multiple_of(place * 32, 32), 32)
                turned[group][to, src] = rows[q * 32:(q + 1) * 32]

    def gram(group, out, first, count):
        rows = pl.ds(out[0], out[1])
        src = pl.ds(first, count)

        @pl.loop(0, NT)
        def _(n):
            cols = pl.ds(pl.multiple_of(n * TILE, TILE), TILE)
            part = jnp.dot(turned[group][rows, src], hidden[group][src, cols], preferred_element_type=F32)
            if group == 0:
                g[n, rows, :] = part
            else:
                g[n, rows, :] += part

    for c in range(CHUNKS):
        for m in (0, 1, 2):
            message(c, m).start()
    tell(0)

    accg[...] = jnp.zeros_like(accg)
    accu[...] = jnp.zeros_like(accu)

    icol = lax.broadcasted_iota(I32, (IN_PAD, IBLK), 1)
    irow = lax.broadcasted_iota(I32, (IN_PAD, IBLK), 0)
    for r in range(32):
        to_y = (1 - yhi) if r % 16 < 8 else yhi
        to_core = core if r < 16 else 1 - core
        owner = to_y * 16 + lax.rem(z + DZ[r % 8], 8) * 2 + to_core
        block = (icol - owner * IN_ROWS == irow) & (irow < IN_ROWS)
        insel[pl.ds(r * IN_PAD, IN_PAD), :] = block.astype(BF16)

    def in_gram(group):
        xb = x[
            t // 2, pl.ds(group * HALF, HALF), pl.ds(pl.multiple_of((t % 2) * IBLK, IBLK), IBLK)
        ]
        xt = lax.dot_general(
            insel[...], xb, (((1,), (1,)), ((), ())), preferred_element_type=F32
        ).astype(BF16)
        part = jnp.dot(xt, xb, preferred_element_type=F32)
        if group == 0:
            gin[...] = part
        else:
            gin[...] += part

    @pl.loop(0, CHUNKS)
    def _(c):
        forwards(c)

        @pl.when(c == 0)
        def _():
            told(0)
            tell(1)

        @pl.when(c == 1)
        def _():
            told(1)
            tell(2)

        @pl.when(c == 2)
        def _():
            told(2)

        message(c, 2).wait_recv()
        for cp in wcopy(c):
            cp.wait()

        @pl.when(c < CHUNKS - 1)
        def _():
            products(c, 0)

        @pl.when(c == CHUNKS - 1)
        def _():
            finish(0)

        @pl.when(c >= 2)
        def _():
            last_forwards(c - 2)

    def arrived(c):
        for m in (4, 7, 8, 9):
            message(c, m).wait_recv()

    def hidden_arrived(group):
        for n in range(NT):
            hcopy(group, n).wait_recv()

    in_gram(0)
    last_forwards(2)

    @pl.loop(0, CHUNKS - 1)
    def _(c):
        arrived(c)
        products(c, 1)

        @pl.when(c == 0)
        def _():
            hidden_arrived(0)
            take_rows(0, 0, 2 * HALF)
            last_forwards(3)

        @pl.when(c == 1)
        def _():
            gram(0, (0, 512), 0, 2 * HALF)

    arrived(CHUNKS - 1)
    finish(1)
    in_gram(1)
    in_sib = pltpu.make_async_remote_copy(
        src_ref=gin.at[pl.ds(256, 256), :], dst_ref=gin_sib, send_sem=in_s.at[0], recv_sem=in_r.at[0],
        device_id=sib, device_id_type=MESH,
    )
    in_sib.start()
    take_rows(1, 0, HALF)
    gram(1, (0, 256), 0, HALF)
    lane = lax.broadcasted_iota(I32, (16, 128), 1)

    def encode(halves, buf):
        codes = []
        for a, vals in enumerate(halves):
            q, code = row_code(vals)
            for b in range(8):
                buf[8 * a + b] = q[:, 128 * b:128 * b + 128]
            codes.append(code)
        buf[16] = jnp.where(lane < 64, codes[0], codes[1]).astype(I16)

    def decode(buf):
        codes = buf[16]
        out = []
        for a in range(2):
            s = row_scale(codes[:, 64 * a:64 * a + 1])
            cat = jnp.concatenate([buf[8 * a + b] for b in range(8)], axis=1)
            out.append(cat.astype(I32).astype(F32) * s)
        return out

    def g_halves(first):
        out = []
        for a in range(2):
            rows = pl.ds(pl.multiple_of(first + 16 * a, 16), 16)
            out.append(jnp.concatenate([g[n, rows, :] for n in range(NT)], axis=1))
        return out

    def ycopy(r):
        return pltpu.make_async_remote_copy(
            src_ref=ys.at[r], dst_ref=yr.at[r], send_sem=y_s.at[r], recv_sem=y_r.at[r],
            device_id=yfar, device_id_type=MESH,
        )

    def far(r):
        k = (r + 1) // 2
        return zpeer(jnp.where(r % 2 == 0, 4 + k, 4 - k))

    def fcopy(k):
        return pltpu.make_async_remote_copy(
            src_ref=fs.at[k], dst_ref=fr.at[k], send_sem=f_s.at[k], recv_sem=f_r.at[k],
            device_id=far(4 + k), device_id_type=MESH,
        )

    def zcopy(r):
        return pltpu.make_async_remote_copy(
            src_ref=zs.at[r], dst_ref=zr.at[r], send_sem=z_s.at[r], recv_sem=z_r.at[r],
            device_id=zpeer(STEP[r]), device_id_type=MESH,
        )

    def izcopy(r):
        return pltpu.make_async_remote_copy(
            src_ref=izs.at[r], dst_ref=izr.at[r], send_sem=iz_s.at[r], recv_sem=iz_r.at[r],
            device_id=far(r), device_id_type=MESH,
        )

    hidden_arrived(1)
    take_rows(1, HALF, HALF)
    gram(1, (0, 256), HALF, HALF)

    @pl.loop(0, 3)
    def _(k):
        encode(g_halves((4 + k) * 32), fs.at[k])
        fcopy(k).start()

    def y_send(r):
        encode(g_halves(r * 32), ys.at[r])
        ycopy(r).start()

    for r in (0, 2, 1):
        y_send(r)

    gram(1, (256, 256), 0, 2 * HALF)
    for r in (5, 6):
        encode(g_halves(256 + r * 32), zs.at[r])
        zcopy(r).start()

    def in_encode(vals, buf, at):
        top = jnp.max(jnp.max(jnp.abs(vals), axis=1, keepdims=True), axis=0, keepdims=True)
        code = jnp.ceil(8.0 * jnp.log2(jnp.maximum(top, 1e-30)))
        q = jnp.round(vals * (jnp.exp2(code * -0.125) * STEPS))
        q = jnp.where(irow == IN_ROWS, code, q).astype(I32).astype(I16)
        for b in range(3):
            buf[at, b] = q[:, 128 * b:128 * b + 128]

    def in_decode(buf, at):
        vals = jnp.concatenate([buf[at, b] for b in range(3)], axis=1).astype(I32).astype(F32)
        return vals * (jnp.exp2(vals[IN_ROWS:IN_ROWS + 1, 0:1] * 0.125) * (1.0 / STEPS))

    in_sib.wait_recv()
    gin[0:256, :] += gin_sib[...]

    @pl.loop(0, 8)
    def _(r):
        in_encode(gin[pl.ds(pl.multiple_of(16 * r, 16), 16), :], iys, r)

    in_y = pltpu.make_async_remote_copy(
        src_ref=iys, dst_ref=iyr, send_sem=in_s.at[1], recv_sem=in_r.at[1],
        device_id=yfar, device_id_type=MESH,
    )
    in_y.start()

    def add(xs, ys):
        return [a + b for a, b in zip(xs, ys)]

    y_send(3)

    def near(r):
        return g_halves(256 + r * 32)

    def from_y(r):
        ycopy(r).wait_recv()
        return decode(yr.at[r])

    def from_z(r):
        zcopy(r).wait_recv()
        return decode(zr.at[r])

    def z_send(r, vals):
        encode(vals, zs.at[r])
        zcopy(r).start()

    z_send(0, add(near(0), from_y(0)))
    z_send(2, add(near(2), from_y(2)))

    total = g_halves(7 * 32)
    for k in range(3):
        fcopy(k).wait_recv()
        total = add(total, decode(fr.at[k]))
    encode(total, ys.at[7])
    ycopy(7).start()

    z_send(1, add(add(near(1), from_y(1)), from_z(0)))
    z_send(4, add(near(4), from_z(2)))

    in_y.wait_recv()

    @pl.loop(0, 7)
    def _(r):
        rows = pl.ds(pl.multiple_of(128 + 16 * r, 16), 16)
        in_encode(gin[rows, :] + in_decode(iyr, r), izs, r)
        izcopy(r).start()

    z_send(3, add(near(3), from_y(3)))

    def put(vals):
        for a in range(2):
            oh_ref[pl.ds(16 * a, 16), :] = vals[a]

    total = near(7)
    for r in (5, 6):
        total = add(total, from_z(r))
    put(add(total, from_y(7)))
    total = in_decode(iyr, 7) + gin[pl.ds(128 + 16 * 7, 16), :]
    for r in range(7):
        izcopy(r).wait_recv()
        total += in_decode(izr, r)
    oin_ref[...] = total[:IN_ROWS] * INV
    total = [oh_ref[pl.ds(16 * a, 16), :] for a in range(2)]
    for r in (1, 4, 3):
        total = add(total, from_z(r))
    put([v * INV for v in total])

    @pl.loop(0, CHUNKS)
    def _(c):
        for m in range(NM):
            message(c, m).wait_send()

    for n in range(NT):
        hcopy(0, n).wait_send()
        hcopy(1, n).wait_send()

    for r in range(7):
        zcopy(r).wait_send()

    @pl.loop(0, 7)
    def _(r):
        izcopy(r).wait_send()

    for r in (0, 1, 2, 3, 7):
        ycopy(r).wait_send()
    for k in range(3):
        fcopy(k).wait_send()
    in_sib.wait_send()
    in_y.wait_send()


def pass_on(a_ref, b_ref, c_ref, d_ref):
    c_ref[...] = a_ref[...]
    d_ref[...] = b_ref[...]


def local(tokens, indices, gate_weight, up_weight):
    vmem = pltpu.VMEM
    dma = pltpu.SemaphoreType.DMA
    whole = pl.BlockSpec(memory_space=pl.ANY)
    out_shape = (
        jax.ShapeDtypeStruct((IN_ROWS, IBLK), F32),
        jax.ShapeDtypeStruct((OWN_ROWS, UNITS), F32),
    )
    factors = pl.pallas_call(
        kernel,
        out_shape=out_shape,
        in_specs=[whole] * 4,
        out_specs=[pl.BlockSpec(memory_space=vmem)] * 2,
        scratch_shapes=[
            vmem((1, SAMP), I32),
            vmem((SEQ, D), BF16),
            vmem((D, UNITS), BF16),
            vmem((D, UNITS), BF16),
            vmem((CHUNKS, ROWS, KC), BF16),
            vmem((NT, ROWS, TILE), F32),
            vmem((NT, ROWS, TILE), F32),
            vmem((2 * HALF, UNITS), BF16),
            vmem((2 * HALF, UNITS), BF16),
            vmem((512, 2 * HALF), BF16),
            vmem((512, 2 * HALF), BF16),
            vmem((NT, 512, TILE), F32),
            vmem((512, IBLK), BF16),
            vmem((512, IBLK), F32),
            vmem((256, IBLK), F32),
            vmem((8, 3, 16, 128), I16),
            vmem((8, 3, 16, 128), I16),
            vmem((7, 3, 16, 128), I16),
            vmem((7, 3, 16, 128), I16),
            vmem((8, 17, 16, 128), I16),
            vmem((8, 17, 16, 128), I16),
            vmem((3, 17, 16, 128), I16),
            vmem((3, 17, 16, 128), I16),
            vmem((7, 17, 16, 128), I16),
            vmem((7, 17, 16, 128), I16),
            dma((2,)),
            dma((CHUNKS, 2)),
            dma((CHUNKS, NM)),
            dma((CHUNKS, NM)),
            dma((2, NT)),
            dma((2, NT)),
            dma((8,)),
            dma((8,)),
            dma((3,)),
            dma((3,)),
            dma((7,)),
            dma((7,)),
            dma((2,)),
            dma((2,)),
            dma((7,)),
            dma((7,)),
            pltpu.SemaphoreType.REGULAR((3, 2)),
        ],
        compiler_params=pltpu.CompilerParams(
            collective_id=0, has_side_effects=True, vmem_limit_bytes=56 * 2**20
        ),
    )(indices.reshape(1, SAMP), tokens, gate_weight, up_weight)
    return pl.pallas_call(
        pass_on,
        out_shape=out_shape,
        in_specs=[pl.BlockSpec(memory_space=vmem)] * 2,
        out_specs=[pl.BlockSpec(memory_space=vmem)] * 2,
    )(*factors)


def solution(mesh):
    in_specs = (
        P(("dp", "tensor"), None),
        P(("dp", "tensor")),
        P(None, "tensor"),
        P(None, "tensor"),
    )
    out_specs = (P("dp", "tensor"), P("dp", "tensor"))
    return jax.shard_map(local, mesh=mesh, in_specs=in_specs, out_specs=out_specs, check_vma=False)
```

time: 69.8 us -> 57.4 us (0.82); the launches traced: 69.7 us -> 56.5 us
  Pallas kernels: 69.1 us -> 55.9 us
    pallas_call x1, Pallas kernels: 63.2 us -> 54.3 us  [local(): pl.pallas_call(kernel, out_shape=out_shape, in_specs=[whole] * 4, out_spe...]
    pallas_call x1, Pallas kernels: 5.84 us -> 1.59 us  [local(): pl.pallas_call(pass_on, out_shape=out_shape, in_specs=[pl.BlockSpec(memor...]
where the time goes in v3:
time: 57.4 us; the launch traced here: 56.5 us
  Pallas kernels  55.9 us (97%)
  between operations  0.64 us (1%)
    pallas_call x1, Pallas kernels, local(): pl.pallas_call(kernel, out_shape=out_shape, in_specs=[whole] * 4, out_spe...  54.3 us
    pallas_call x1, Pallas kernels, local(): pl.pallas_call(pass_on, out_shape=out_shape, in_specs=[pl.BlockSpec(memor...  1.59 us

profile of v3, /device:TPU:1, one launch (start us, length us, event | category | flops | bytes accessed | tf_op | source)
XLA Modules:
  0.0 56.5 jit_solution(131477726508174259)
XLA Ops:
  0.6 54.3 %shard_map.59 = (f32[12,384]{1,0:T(8,128)}, f32[32,1024]{1,0:T(8,128)}) custom-call(s32[1,64]{1,0:T(1,128)} %bitcast.1, bf16[128,3072]{1,0:T(8,128)(2,1)} %tok_hbm.1, bf16[3072,1024]{1,0:T(8,128)(2,1)} %wg_hbm.1, bf16[3072,1024]{1,0:T(8,128)(2,1)} %wu_hbm.1), custom_call_target="tpu_custom_call" | custom-call | tf_op jit(solution)/shard_map/pallas_call | solution.py:518
  54.9 1.6 %shard_map.60 = (f32[12,384]{1,0:T(8,128)}, f32[32,1024]{1,0:T(8,128)}) custom-call(f32[12,384]{1,0:T(8,128)} %get-tuple-element.4.a_ref, f32[32,1024]{1,0:T(8,128)} %get-tuple-element.5.b_ref), custom_call_target="tpu_custom_call" | custom-call | tf_op jit(solution)/shard_map/pallas_call | solution.py:571

commit v4 on v3

--- a/solution.py
+++ b/solution.py
@@ -43,7 +43,9 @@
     (S_YXM, S_YX2, 32, 16, "xp"),
     (S_YXP, S_YX2, 48, 16, "xm"),
 )
-NM = len(MSGS)
+ARRIVAL = (0, 1, 2, 3, 6, 4, 5, 6, 6, 6)
+LAST_ROWS = (S_X2 + 32, 96)
+SENT_ROWS = sum(msg[3] for msg in MSGS)
 
 
 def row_code(vals):
@@ -114,13 +116,16 @@
 
     pl.semaphore_wait(barrier, len(peers))
 
+    def wait_for(ref, sem):
+        pltpu.make_async_copy(ref, ref, sem).wait()
+
     def message(c, m):
         src, dst, first, n, way = MSGS[m]
         return pltpu.make_async_remote_copy(
             src_ref=x.at[c, pl.ds(src + first, n), :],
             dst_ref=x.at[c, pl.ds(dst + first, n), :],
-            send_sem=ag_s.at[c, m],
-            recv_sem=ag_r.at[c, m],
+            send_sem=ag_s.at[c],
+            recv_sem=ag_r.at[c, ARRIVAL[m]],
             device_id=where[way],
             device_id_type=MESH,
         )
@@ -281,8 +286,7 @@
             last_forwards(c - 2)
 
     def arrived(c):
-        for m in (4, 7, 8, 9):
-            message(c, m).wait_recv()
+        wait_for(x.at[c, pl.ds(*LAST_ROWS), :], ag_r.at[c, 6])
 
     def hidden_arrived(group):
         for n in range(NT):
@@ -345,7 +349,7 @@
 
     def ycopy(r):
         return pltpu.make_async_remote_copy(
-            src_ref=ys.at[r], dst_ref=yr.at[r], send_sem=y_s.at[r], recv_sem=y_r.at[r],
+            src_ref=ys.at[r], dst_ref=yr.at[r], send_sem=y_s, recv_sem=y_r.at[r],
             device_id=yfar, device_id_type=MESH,
         )
 
@@ -355,19 +359,19 @@
 
     def fcopy(k):
         return pltpu.make_async_remote_copy(
-            src_ref=fs.at[k], dst_ref=fr.at[k], send_sem=f_s.at[k], recv_sem=f_r.at[k],
+            src_ref=fs.at[k], dst_ref=fr.at[k], send_sem=f_s, recv_sem=f_r,
             device_id=far(4 + k), device_id_type=MESH,
         )
 
     def zcopy(r):
         return pltpu.make_async_remote_copy(
-            src_ref=zs.at[r], dst_ref=zr.at[r], send_sem=z_s.at[r], recv_sem=z_r.at[r],
+            src_ref=zs.at[r], dst_ref=zr.at[r], send_sem=z_s, recv_sem=z_r.at[r],
             device_id=zpeer(STEP[r]), device_id_type=MESH,
         )
 
     def izcopy(r):
         return pltpu.make_async_remote_copy(
-            src_ref=izs.at[r], dst_ref=izr.at[r], send_sem=iz_s.at[r], recv_sem=iz_r.at[r],
+            src_ref=izs.at[r], dst_ref=izr.at[r], send_sem=iz_s, recv_sem=iz_r,
             device_id=far(r), device_id_type=MESH,
         )
 
@@ -437,12 +441,20 @@
         encode(vals, zs.at[r])
         zcopy(r).start()
 
+    @pl.loop(0, CHUNKS)
+    def _(c):
+        wait_for(x.at[c, pl.ds(0, SENT_ROWS), :], ag_s.at[c])
+
+    for n in range(NT):
+        hcopy(0, n).wait_send()
+        hcopy(1, n).wait_send()
+
     z_send(0, add(near(0), from_y(0)))
     z_send(2, add(near(2), from_y(2)))
 
     total = g_halves(7 * 32)
+    wait_for(fr, f_r)
     for k in range(3):
-        fcopy(k).wait_recv()
         total = add(total, decode(fr.at[k]))
     encode(total, ys.at[7])
     ycopy(7).start()
@@ -469,8 +481,8 @@
         total = add(total, from_z(r))
     put(add(total, from_y(7)))
     total = in_decode(iyr, 7) + gin[pl.ds(128 + 16 * 7, 16), :]
+    wait_for(izr, iz_r)
     for r in range(7):
-        izcopy(r).wait_recv()
         total += in_decode(izr, r)
     oin_ref[...] = total[:IN_ROWS] * INV
     total = [oh_ref[pl.ds(16 * a, 16), :] for a in range(2)]
@@ -478,26 +490,10 @@
         total = add(total, from_z(r))
     put([v * INV for v in total])
 
-    @pl.loop(0, CHUNKS)
-    def _(c):
-        for m in range(NM):
-            message(c, m).wait_send()
-
-    for n in range(NT):
-        hcopy(0, n).wait_send()
-        hcopy(1, n).wait_send()
-
-    for r in range(7):
-        zcopy(r).wait_send()
-
-    @pl.loop(0, 7)
-    def _(r):
-        izcopy(r).wait_send()
-
-    for r in (0, 1, 2, 3, 7):
-        ycopy(r).wait_send()
-    for k in range(3):
-        fcopy(k).wait_send()
+    wait_for(zs, z_s)
+    wait_for(izs, iz_s)
+    wait_for(ys.at[pl.ds(0, 5)], y_s)
+    wait_for(fs, f_s)
     in_sib.wait_send()
     in_y.wait_send()
 
@@ -548,20 +544,20 @@
             vmem((7, 17, 16, 128), I16),
             dma((2,)),
             dma((CHUNKS, 2)),
-            dma((CHUNKS, NM)),
-            dma((CHUNKS, NM)),
+            dma((CHUNKS,)),
+            dma((CHUNKS, 7)),
             dma((2, NT)),
             dma((2, NT)),
+            dma,
             dma((8,)),
-            dma((8,)),
-            dma((3,)),
-            dma((3,)),
-            dma((7,)),
+            dma,
+            dma,
+            dma,
             dma((7,)),
             dma((2,)),
             dma((2,)),
-            dma((7,)),
-            dma((7,)),
+            dma,
+            dma,
             pltpu.SemaphoreType.REGULAR((3, 2)),
         ],
         compiler_params=pltpu.CompilerParams(

time: 57.4 us -> 56.5 us (0.984)
  Pallas kernels: 55.9 us -> 55 us
    pallas_call x1, Pallas kernels: 54.3 us -> 53.4 us  [local(): pl.pallas_call(kernel, out_shape=out_shape, in_specs=[whole] * 4, out_spe...]
where the time goes in v4:
time: 56.5 us; the launch traced here: 55.7 us
  Pallas kernels  55 us (97%)
  between operations  0.64 us (1%)
    pallas_call x1, Pallas kernels, local(): pl.pallas_call(kernel, out_shape=out_shape, in_specs=[whole] * 4, out_spe...  53.4 us
    pallas_call x1, Pallas kernels, local(): pl.pallas_call(pass_on, out_shape=out_shape, in_specs=[pl.BlockSpec(memor...  1.59 us

profile of v4, /device:TPU:1, one launch (start us, length us, event | category | flops | bytes accessed | tf_op | source)
XLA Modules:
  0.0 55.7 jit_solution(11329524039825699581)
XLA Ops:
  0.6 53.4 %shard_map.59 = (f32[12,384]{1,0:T(8,128)}, f32[32,1024]{1,0:T(8,128)}) custom-call(s32[1,64]{1,0:T(1,128)} %bitcast.1, bf16[128,3072]{1,0:T(8,128)(2,1)} %tok_hbm.1, bf16[3072,1024]{1,0:T(8,128)(2,1)} %wg_hbm.1, bf16[3072,1024]{1,0:T(8,128)(2,1)} %wu_hbm.1), custom_call_target="tpu_custom_call" | custom-call | tf_op jit(solution)/shard_map/pallas_call | solution.py:514
  54.1 1.6 %shard_map.60 = (f32[12,384]{1,0:T(8,128)}, f32[32,1024]{1,0:T(8,128)}) custom-call(f32[12,384]{1,0:T(8,128)} %get-tuple-element.4.a_ref, f32[32,1024]{1,0:T(8,128)} %get-tuple-element.5.b_ref), custom_call_target="tpu_custom_call" | custom-call | tf_op jit(solution)/shard_map/pallas_call | solution.py:567

commit v5 on v4

--- a/solution.py
+++ b/solution.py
@@ -377,19 +377,21 @@
 
     hidden_arrived(1)
     take_rows(1, HALF, HALF)
-    gram(1, (0, 256), HALF, HALF)
+    def y_send(r):
+        encode(g_halves(r * 32), ys.at[r])
+        ycopy(r).start()
+
+    gram(1, (0, 128), HALF, HALF)
+    y_send(0)
+    y_send(2)
+    gram(1, (128, 128), HALF, HALF)
 
     @pl.loop(0, 3)
     def _(k):
         encode(g_halves((4 + k) * 32), fs.at[k])
         fcopy(k).start()
 
-    def y_send(r):
-        encode(g_halves(r * 32), ys.at[r])
-        ycopy(r).start()
-
-    for r in (0, 2, 1):
-        y_send(r)
+    y_send(1)
 
     gram(1, (256, 256), 0, 2 * HALF)
     for r in (5, 6):

time: 56.5 us -> 56.2 us (level); the launches traced: 55.7 us -> 56.1 us
  no operation moved by 1% of the time
where the time goes in v5:
time: 56.2 us; the launch traced here: 56.1 us
  Pallas kernels  55.4 us (99%)
  between operations  0.64 us (1%)
    pallas_call x1, Pallas kernels, local(): pl.pallas_call(kernel, out_shape=out_shape, in_specs=[whole] * 4, out_spe...  53.9 us
    pallas_call x1, Pallas kernels, local(): pl.pallas_call(pass_on, out_shape=out_shape, in_specs=[pl.BlockSpec(memor...  1.59 us

profile of v5, /device:TPU:1, one launch (start us, length us, event | category | flops | bytes accessed | tf_op | source)
XLA Modules:
  0.0 56.1 jit_solution(6413189066306137962)
XLA Ops:
  0.6 53.9 %shard_map.59 = (f32[12,384]{1,0:T(8,128)}, f32[32,1024]{1,0:T(8,128)}) custom-call(s32[1,64]{1,0:T(1,128)} %bitcast.1, bf16[128,3072]{1,0:T(8,128)(2,1)} %tok_hbm.1, bf16[3072,1024]{1,0:T(8,128)(2,1)} %wg_hbm.1, bf16[3072,1024]{1,0:T(8,128)(2,1)} %wu_hbm.1), custom_call_target="tpu_custom_call" | custom-call | tf_op jit(solution)/shard_map/pallas_call | solution.py:516
  54.5 1.6 %shard_map.60 = (f32[12,384]{1,0:T(8,128)}, f32[32,1024]{1,0:T(8,128)}) custom-call(f32[12,384]{1,0:T(8,128)} %get-tuple-element.4.a_ref, f32[32,1024]{1,0:T(8,128)} %get-tuple-element.5.b_ref), custom_call_target="tpu_custom_call" | custom-call | tf_op jit(solution)/shard_map/pallas_call | solution.py:569

commit v6 on v5

--- a/solution.py
+++ b/solution.py
@@ -462,7 +462,6 @@
     ycopy(7).start()
 
     z_send(1, add(add(near(1), from_y(1)), from_z(0)))
-    z_send(4, add(near(4), from_z(2)))
 
     in_y.wait_recv()
 
@@ -471,6 +470,8 @@
         rows = pl.ds(pl.multiple_of(128 + 16 * r, 16), 16)
         in_encode(gin[rows, :] + in_decode(iyr, r), izs, r)
         izcopy(r).start()
+
+    z_send(4, add(near(4), from_z(2)))
 
     z_send(3, add(near(3), from_y(3)))
 

time: 56.2 us -> 56.6 us (level)
  the two profiles are of different devices: /device:TPU:1 before, /device:TPU:8 now
where the time goes in v6:
time: 56.6 us; the launch traced here: 56.4 us
  Pallas kernels  55.8 us (99%)
  between operations  0.64 us (1%)
    pallas_call x1, Pallas kernels, local(): pl.pallas_call(kernel, out_shape=out_shape, in_specs=[whole] * 4, out_spe...  54.2 us
    pallas_call x1, Pallas kernels, local(): pl.pallas_call(pass_on, out_shape=out_shape, in_specs=[pl.BlockSpec(memor...  1.59 us

profile of v6, /device:TPU:8, one launch (start us, length us, event | category | flops | bytes accessed | tf_op | source)
XLA Modules:
  0.0 56.4 jit_solution(8506237259782028708)
XLA Ops:
  0.6 54.2 %shard_map.59 = (f32[12,384]{1,0:T(8,128)}, f32[32,1024]{1,0:T(8,128)}) custom-call(s32[1,64]{1,0:T(1,128)} %bitcast.1, bf16[128,3072]{1,0:T(8,128)(2,1)} %tok_hbm.1, bf16[3072,1024]{1,0:T(8,128)(2,1)} %wg_hbm.1, bf16[3072,1024]{1,0:T(8,128)(2,1)} %wu_hbm.1), custom_call_target="tpu_custom_call" | custom-call | tf_op jit(solution)/shard_map/pallas_call | solution.py:517
  54.8 1.6 %shard_map.60 = (f32[12,384]{1,0:T(8,128)}, f32[32,1024]{1,0:T(8,128)}) custom-call(f32[12,384]{1,0:T(8,128)} %get-tuple-element.4.a_ref, f32[32,1024]{1,0:T(8,128)} %get-tuple-element.5.b_ref), custom_call_target="tpu_custom_call" | custom-call | tf_op jit(solution)/shard_map/pallas_call | solution.py:570
